TPU v7x, 256 devices: a whole 4x4x8 slice. The times are simulated.
256 devices in a mesh: chan: 32 (over y, x, core), band: 8 (over z).
Axes of the slice: x: 4, y: 4, z: 8, core: 2. Of those that a mesh axis runs over, the one named last changes fastest.
Arguments:
- spectra: bfloat16 [2, 30, 512, 8192], P(None, None, 'chan', 'band'), may hold values from -6 to 6
- source_block: int32 [1], replicated, may hold values from 0 to 127
- segment_flags: int32 [30], replicated, may hold values from 0 to 1, as said below
Outputs:
- correlations: float32 [64, 8, 1024, 1024], P(None, 'band', 'chan')
Inputs may be any that keep to these rules, and one draw needn't show every extreme that they name: `segment_flags`: at least one segment is valid.
All inputs are finite; a program needn't handle non-finite values.
Results may differ from a plain program's by a relative error of at most 0.0037.
Values may be sent and summed in bfloat16 or wider, within the bound.
A program may use at most 128 MiB of HBM per device.

v0:
```python
import math
import jax
import jax.numpy as jnp
from jax import lax
from jax.sharding import PartitionSpec as P

LAGS = 1024
F = 512
SRC = 64
RB = 1024


def spread(block, axis, owner):
    block = jnp.where(lax.axis_index(axis) == owner, block, jnp.zeros_like(block))
    return lax.psum(block, axis)


def lag_table():
    frequency = jnp.arange(F, dtype=jnp.int32)[:, None]
    shifted_lag = jnp.arange(LAGS, dtype=jnp.int32)[None, :] - LAGS // 2
    phase_index = frequency * shifted_lag % LAGS
    phase_angle = 2.0 * math.pi / LAGS * phase_index.astype(jnp.float32)
    weight = jnp.where(frequency == 0, 1.0, 2.0).astype(jnp.float32) / jnp.sqrt(jnp.float32(2 * F))
    cosine_component = weight * jnp.cos(phase_angle)
    sin_part = -weight * jnp.sin(phase_angle)
    return jnp.stack([cosine_component, sin_part], axis=1).astype(jnp.bfloat16)


def stack_segment_windows(source, receiver_traces, valid_mask, valid_window_count):
    masked = source * valid_mask[None, :, None, None]
    left_real = jnp.concatenate([masked[0], masked[1]], axis=0)
    left_imaginary = jnp.concatenate([masked[1], -masked[0]], axis=0)
    left_operand = jnp.concatenate([left_real, left_imaginary], axis=2)
    bins = receiver_traces.shape[2]
    width = receiver_traces.shape[3]
    right_side = receiver_traces.reshape(2 * receiver_traces.shape[1], bins, width)
    summed = lax.dot_general(
        left_operand, right_side, (((0,), (0,)), ((1,), (1,))), preferred_element_type=jnp.float32
    )
    cross_spectrum_product = (summed / valid_window_count).astype(jnp.bfloat16)
    return cross_spectrum_product.reshape(bins, 2, SRC, width)


def local(spectra, source_block, segment_flags):
    first_channel = source_block[0] * SRC
    owner_band = first_channel // RB
    offset = first_channel - owner_band * RB
    local_source = lax.dynamic_slice_in_dim(spectra, offset, SRC, 3)
    source = spread(local_source, "band", owner_band)
    valid_mask = segment_flags.astype(jnp.bfloat16)
    valid_window_count = jnp.sum(segment_flags).astype(jnp.float32)
    lag_weights = lag_table()
    cross_spectrum_product = stack_segment_windows(source, spectra, valid_mask, valid_window_count)
    lagged_correlation = lax.dot_general(
        lax.all_to_all(cross_spectrum_product, "chan", split_axis=3, concat_axis=0, tiled=True),
        lag_weights,
        (((0, 1), (0, 1)), ((), ())),
        preferred_element_type=jnp.float32,
    )
    return lagged_correlation[:, None]


def solution(mesh):
    return jax.shard_map(
        local,
        mesh=mesh,
        in_specs=(P(None, None, "chan", "band"), P(), P()),
        out_specs=P(None, "band", "chan", None),
        check_vma=False,
    )
```

profile of v0, /device:TPU:32, one launch (start us, length us, event | category | flops | bytes accessed | tf_op | source)
XLA Modules:
  0.0 248.0 jit_solution(11593618754978882445)
XLA Ops:
  6.5 0.0 copy-start
  6.5 0.0 all-reduce.2.cloned.1.call-start
  7.4 0.7 copy-done
  8.1 0.1 constant_dynamic-slice_fusion
  8.2 0.8 copy_select_fusion
  9.0 0.0 all-reduce.2.cloned.1.call-update
  9.0 1.4 fusion.20
  11.0 73.7 %all-reduce.2.cloned.1.call-done = bf16[2,30,16,64]{3,1,2,0:T(8,128)(2,1)} async-done(((bf16[2,30,16,64]{3,1,2,0:T(8,128)(2,1)}), bf16[2,30,16,64]{3,1,2,0:T(8,128)(2,1)}) %all-reduce.2.cloned.1.call-update) | async-done | bytes 122896 | tf_op jit(solution)/shard_map/psum | solution.py:15
  84.7 1.0 broadcast_multiply_fusion
  85.8 5.1 %divide_convert_fusion = bf16[16,128,1024]{2,1,0:T(8,128)(2,1)} fusion(f32[]{:T(128)S(6)} %convert_element_type.27, bf16[60,16,1024]{2,1,0:T(8,128)(2,1)S(1)} %bitcast.25, bf16[30,16,64]{2,0,1:T(8,128)(2,1)S(1)} %fusion.19, bf16[30,16,64]{2,0,1:T(8,128)(2,1)S(1)} %get-tuple-element.6, bf16[30,16,64]{2,0,1:T(8,128)(2,1)S(1)} %get-tuple-element.5), kind=kOutput, calls=%fused_computation | convolution fusion | flops 256835584 | bytes 6344708 | tf_op jit(solution)/shard_map/dot_general | solution.py:37
  90.9 20.3 %copy.16 = bf16[16,2,64,1024]{2,1,0,3:T(2,128)(2,1)} copy(bf16[16,2,64,1024]{3,2,1,0:T(8,128)(2,1)} %bitcast.30) | data formatting | bytes 8388608 | tf_op jit(solution)/shard_map/reshape | solution.py:41
  111.2 13.9 %reshape.165 = bf16[32,2,32768]{2,1,0:T(2,128)(2,1)} reshape(bf16[1024,16,2,64]{3,2,1,0:T(2,128)(2,1)} %bitcast.26) | data formatting | bytes 8388608
  125.1 7.4 %all-to-all-start = ((bf16[32,2,32768]{2,1,0:T(2,128)(2,1)}), bf16[32,2,32768]{2,1,0:T(2,128)(2,1)}, u32[]{:S(2)}, u32[]{:S(2)}) async-start(bf16[32,2,32768]{2,1,0:T(2,128)(2,1)} %reshape.165), calls=%async_computation | async-start | bytes 8388608 | tf_op jit(solution)/shard_map/all_to_all | solution.py:55
  132.5 9.4 %multiply_convert_fusion.1 = (bf16[512,1,1024]{2,0,1:T(8,128)(2,1)S(1)}, bf16[512,1,1024]{2,0,1:T(8,128)(2,1)}) fusion(s32[1024]{0:T(1024)S(1)} %iota_add_fusion, f32[512]{0:T(512)S(1)} %get-tuple-element.11, f32[512]{0:T(512)S(1)} %get-tuple-element.12), kind=kLoop, calls=%fused_computation.13 | loop fusion | flops 9437184 | bytes 2105344 | tf_op jit(solution)/shard_map/convert
  141.9 43.9 %all-to-all-done = bf16[32,2,32768]{2,1,0:T(2,128)(2,1)} async-done(((bf16[32,2,32768]{2,1,0:T(2,128)(2,1)}), bf16[32,2,32768]{2,1,0:T(2,128)(2,1)}, u32[]{:S(2)}, u32[]{:S(2)}) %all-to-all-start) | async-done | bytes 4194336 | tf_op jit(solution)/shard_map/all_to_all | solution.py:55
  185.8 13.6 %reshape.166 = bf16[1024,16,2,64]{3,2,1,0:T(2,128)(2,1)} reshape(bf16[32,2,32768]{2,1,0:T(2,128)(2,1)} %all-to-all-done) | data formatting | bytes 8388608
  199.4 9.8 %copy.17 = bf16[16,2,64,1024]{2,3,1,0:T(8,128)(2,1)} copy(bf16[16,2,64,1024]{2,1,0,3:T(2,128)(2,1)} %bitcast.27) | data formatting | bytes 8388608 | tf_op jit(solution)/shard_map/all_to_all | solution.py:55
  209.2 9.5 %copy.18 = bf16[32,16,2,64,32]{3,4,2,1,0:T(8,128)(2,1)} copy(bf16[32,16,2,64,32]{3,4,0,2,1:T(8,128)(2,1)} %bitcast.28) | data formatting | bytes 8388608 | tf_op jit(solution)/shard_map/all_to_all | solution.py:55
  218.7 12.0 %copy.19 = bf16[512,2,64,32]{0,3,1,2:T(8,128)(2,1)} copy(bf16[512,2,64,32]{2,3,1,0:T(8,128)(2,1)} %bitcast.29) | data formatting | bytes 8388608 | tf_op jit(solution)/shard_map/all_to_all | solution.py:55
  230.7 10.4 %convolution_bitcast_fusion = f32[64,1,32,1024]{3,2,1,0:T(8,128)} fusion(bf16[512,2,64,32]{0,3,1,2:T(8,128)(2,1)} %copy.19, bf16[512,1,1024]{2,0,1:T(8,128)(2,1)} %get-tuple-element.8, bf16[512,1,1024]{2,0,1:T(8,128)(2,1)S(1)} %get-tuple-element.7), kind=kOutput, calls=%fused_computation.1 | convolution fusion | flops 4296015872 | bytes 14680064 | tf_op jit(solution)/shard_map/dot_general | solution.py:54
  (4 shorter events, 0.0 us)
Async XLA Ops:
  6.5 1.6 copy-start
  6.5 78.1 %all-reduce.2.cloned.1.call-start = ((), (), s32[]{:S(2)}) async-start(), calls=%async_computation.1 | async-start | bytes 524288 | tf_op jit(solution)/shard_map/psum | solution.py:15
  125.1 60.7 %all-to-all-start = ((bf16[32,2,32768]{2,1,0:T(2,128)(2,1)}), bf16[32,2,32768]{2,1,0:T(2,128)(2,1)}, u32[]{:S(2)}, u32[]{:S(2)}) async-start(bf16[32,2,32768]{2,1,0:T(2,128)(2,1)} %reshape.165), calls=%async_computation | async-start | bytes 8388608 | tf_op jit(solution)/shard_map/all_to_all | solution.py:55
Sparse Core Ops, SparseCore 0:
  9.7 74.9 all-reduce.1
where the time goes:
time: 250 us; the launch traced here: 248 us
  waiting for transfers between devices  118 us (47%)
  local copies, waits for them, and re-layouts  80 us (32%)
  matrix products  15.5 us (6%)
  between operations  14.8 us (6%)
  other arithmetic  12.5 us (5%)
  starting transfers between devices  7.4 us (3%)
    psum x1, waiting for transfers between devices, spread(): return lax.psum(block, axis)  73.7 us
    all_to_all x1, waiting for transfers between devices, local(): lax.all_to_all(cross_spectrum_product, 'chan', split_axis=3, concat_axis=...  43.9 us
    all_to_all x3, local copies, waits for them, and re-layouts, local(): lax.all_to_all(cross_spectrum_product, 'chan', split_axis=3, concat_axis=...  31.3 us
    unnamed x4, local copies, waits for them, and re-layouts  28.3 us
    reshape x1, local copies, waits for them, and re-layouts, stack_segment_windows(): return cross_spectrum_product.reshape(bins, 2, SRC, width)  20.3 us
    dot_general x1, matrix products, local(): lax.dot_general(lax.all_to_all(cross_spectrum_product, 'chan', split_axis...  10.4 us
    another operation x1, other arithmetic  9.35 us
    all_to_all x1, starting transfers between devices, local(): lax.all_to_all(cross_spectrum_product, 'chan', split_axis=3, concat_axis=...  7.4 us
  transfers between devices with their start and end apart: 2, of which 2 were waited for; matrix products, arithmetic and copies ran while one was open for 4% of the time, Pallas kernels for 0%

commit v1 on v0

--- a/solution.py
+++ b/solution.py
@@ -12,7 +12,7 @@
 
 def spread(block, axis, owner):
     block = jnp.where(lax.axis_index(axis) == owner, block, jnp.zeros_like(block))
-    return lax.psum(block, axis)
+    return jnp.sum(lax.all_gather(block, axis), axis=0)
 
 
 def lag_table():

time: 250 us -> 193 us (0.77)
  waiting for transfers between devices: 118 us -> 44.6 us
  blocking collectives: 0 us -> 31.9 us
  between operations: 14.8 us -> 1.41 us
    psum x1 -> x0, waiting for transfers between devices: 73.7 us -> none  [spread(): return lax.psum(block, axis)]
    all_gather x0 -> x1, blocking collectives: none -> 31.9 us  [spread(): return jnp.sum(lax.all_gather(block, axis), axis=0)]
  transfers between devices with their start and end apart: 2 -> 1, of which waited for: 2 -> 1; matrix products, arithmetic and copies ran while one was open for 4% -> 5% of each run, Pallas kernels for 0% -> 0%
where the time goes in v1:
time: 193 us; the launch traced here: 191 us
  local copies, waits for them, and re-layouts  79.2 us (41%)
  waiting for transfers between devices  44.6 us (23%)
  blocking collectives  31.9 us (17%)
  matrix products  15.6 us (8%)
  other arithmetic  11 us (6%)
  starting transfers between devices  7.63 us (4%)
    all_to_all x1, waiting for transfers between devices, local(): lax.all_to_all(cross_spectrum_product, 'chan', split_axis=3, concat_axis=...  44.6 us
    all_gather x1, blocking collectives, spread(): return jnp.sum(lax.all_gather(block, axis), axis=0)  31.9 us
    all_to_all x3, local copies, waits for them, and re-layouts, local(): lax.all_to_all(cross_spectrum_product, 'chan', split_axis=3, concat_axis=...  31.4 us
    unnamed x4, local copies, waits for them, and re-layouts  27.5 us
    reshape x1, local copies, waits for them, and re-layouts, stack_segment_windows(): return cross_spectrum_product.reshape(bins, 2, SRC, width)  20.3 us
    dot_general x1, matrix products, local(): lax.dot_general(lax.all_to_all(cross_spectrum_product, 'chan', split_axis...  8.92 us
    another operation x1, other arithmetic  8.65 us
    all_to_all x1, starting transfers between devices, local(): lax.all_to_all(cross_spectrum_product, 'chan', split_axis=3, concat_axis=...  7.63 us
  transfers between devices with their start and end apart: 1, of which 1 were waited for; matrix products, arithmetic and copies ran while one was open for 5% of the time, Pallas kernels for 0%

profile of v1, /device:TPU:32, one launch (start us, length us, event | category | flops | bytes accessed | tf_op | source)
XLA Modules:
  0.0 191.2 jit_solution(4933125321703029951)
XLA Ops:
  0.0 0.0 copy-start
  0.7 1.1 dynamic-slice_select_fusion
  1.8 31.9 %all-gather = bf16[16,30,16,64]{3,2,1,0:T(8,128)(2,1)S(1)} all-gather(bf16[2,30,16,64]{3,2,1,0:T(8,128)(2,1)S(1)} %dynamic-slice_select_fusion), channel_id=2, replica_groups=mesh['chan'=32,'band'=8] {'band'}, dimensions={0}, use_global_device_ids=true | all-gather | bytes 1105920 | tf_op jit(solution)/shard_map/all_gather | solution.py:15
  33.7 0.0 copy-done
  33.7 0.6 fusion.20
  34.3 0.5 reduce_sum.21
  34.8 0.1 copy_multiply_fusion
  35.6 6.7 %divide_convert_fusion = bf16[16,128,1024]{2,1,0:T(8,128)(2,1)} fusion(f32[]{:T(128)S(6)} %convert_element_type.29, bf16[60,16,1024]{2,1,0:T(8,128)(2,1)} %bitcast.32, bf16[30,16,64]{2,0,1:T(8,128)(2,1)S(1)} %fusion.19, bf16[30,16,64]{2,0,1:T(8,128)(2,1)S(1)} %get-tuple-element.6, bf16[30,16,64]{2,0,1:T(8,128)(2,1)S(1)} %get-tuple-element.5), kind=kOutput, calls=%fused_computation | convolution fusion | flops 256835584 | bytes 6344708 | tf_op jit(solution)/shard_map/dot_general | solution.py:37
  42.3 20.3 %copy.14 = bf16[16,2,64,1024]{2,1,0,3:T(2,128)(2,1)} copy(bf16[16,2,64,1024]{3,2,1,0:T(8,128)(2,1)} %bitcast.31) | data formatting | bytes 8388608 | tf_op jit(solution)/shard_map/reshape | solution.py:41
  62.5 13.9 %reshape.166 = bf16[32,2,32768]{2,1,0:T(2,128)(2,1)} reshape(bf16[1024,16,2,64]{3,2,1,0:T(2,128)(2,1)} %bitcast.26) | data formatting | bytes 8388608
  76.4 7.6 %all-to-all-start = ((bf16[32,2,32768]{2,1,0:T(2,128)(2,1)}), bf16[32,2,32768]{2,1,0:T(2,128)(2,1)}, u32[]{:S(2)}, u32[]{:S(2)}) async-start(bf16[32,2,32768]{2,1,0:T(2,128)(2,1)} %reshape.166), calls=%async_computation | async-start | bytes 8388608 | tf_op jit(solution)/shard_map/all_to_all | solution.py:55
  84.1 8.6 %multiply_convert_fusion.1 = (bf16[512,1,1024]{2,0,1:T(8,128)(2,1)S(1)}, bf16[512,1,1024]{2,0,1:T(8,128)(2,1)S(1)}) fusion(s32[1024]{0:T(1024)S(1)} %iota_add_fusion, f32[512]{0:T(512)S(1)} %get-tuple-element.11, f32[512]{0:T(512)S(1)} %get-tuple-element.12), kind=kLoop, calls=%fused_computation.13 | loop fusion | flops 9437184 | bytes 2105344 | tf_op jit(solution)/shard_map/convert.1
  92.7 44.6 %all-to-all-done = bf16[32,2,32768]{2,1,0:T(2,128)(2,1)} async-done(((bf16[32,2,32768]{2,1,0:T(2,128)(2,1)}), bf16[32,2,32768]{2,1,0:T(2,128)(2,1)}, u32[]{:S(2)}, u32[]{:S(2)}) %all-to-all-start) | async-done | bytes 4194336 | tf_op jit(solution)/shard_map/all_to_all | solution.py:55
  137.3 13.6 %reshape.167 = bf16[1024,16,2,64]{3,2,1,0:T(2,128)(2,1)} reshape(bf16[32,2,32768]{2,1,0:T(2,128)(2,1)} %all-to-all-done) | data formatting | bytes 8388608
  151.0 9.8 %copy.15 = bf16[16,2,64,1024]{2,3,1,0:T(8,128)(2,1)} copy(bf16[16,2,64,1024]{2,1,0,3:T(2,128)(2,1)} %bitcast.27) | data formatting | bytes 8388608 | tf_op jit(solution)/shard_map/all_to_all | solution.py:55
  160.8 9.5 %copy.16 = bf16[32,16,2,64,32]{3,4,2,1,0:T(8,128)(2,1)} copy(bf16[32,16,2,64,32]{3,4,0,2,1:T(8,128)(2,1)} %bitcast.28) | data formatting | bytes 8388608 | tf_op jit(solution)/shard_map/all_to_all | solution.py:55
  170.2 12.1 %copy.17 = bf16[512,2,64,32]{0,3,1,2:T(8,128)(2,1)} copy(bf16[512,2,64,32]{2,3,1,0:T(8,128)(2,1)} %bitcast.29) | data formatting | bytes 8388608 | tf_op jit(solution)/shard_map/all_to_all | solution.py:55
  182.3 8.9 %convolution_bitcast_fusion = f32[64,1,32,1024]{3,2,1,0:T(8,128)} fusion(bf16[512,2,64,32]{0,3,1,2:T(8,128)(2,1)} %copy.17, bf16[512,1,1024]{2,0,1:T(8,128)(2,1)S(1)} %get-tuple-element.8, bf16[512,1,1024]{2,0,1:T(8,128)(2,1)S(1)} %get-tuple-element.7), kind=kOutput, calls=%fused_computation.1 | convolution fusion | flops 4296015872 | bytes 14680064 | tf_op jit(solution)/shard_map/dot_general | solution.py:54
  (4 shorter events, 0.0 us)
Async XLA Ops:
  0.0 33.7 %copy-start = (s32[30]{0:T(128)S(1)}, s32[30]{0:T(128)}, u32[]{:S(2)}) copy-start(s32[30]{0:T(128)} %param.5) | copy-start | bytes 364
  76.4 60.9 %all-to-all-start = ((bf16[32,2,32768]{2,1,0:T(2,128)(2,1)}), bf16[32,2,32768]{2,1,0:T(2,128)(2,1)}, u32[]{:S(2)}, u32[]{:S(2)}) async-start(bf16[32,2,32768]{2,1,0:T(2,128)(2,1)} %reshape.166), calls=%async_computation | async-start | bytes 8388608 | tf_op jit(solution)/shard_map/all_to_all | solution.py:55
